TPU v7x, 32 devices: a whole 2x2x4 slice. The times are simulated.
32 devices in a mesh: seq: 8 (over y, x, core), dp: 4 (over z).
Axes of the slice: x: 2, y: 2, z: 4, core: 2. Of those that a mesh axis runs over, the one named last changes fastest.
Arguments:
- normed_input: bfloat16 [4, 1024, 5376], P('dp', 'seq'), may hold values from -6 to 6
- q_base: bfloat16 [4, 1024, 2048], P('dp', 'seq'), may hold values from -6 to 6
- k_base: bfloat16 [4, 1024, 1024], P('dp', 'seq'), may hold values from -6 to 6
- v_base: bfloat16 [4, 1024, 1024], P('dp', 'seq'), may hold values from -6 to 6
- d_attn: bfloat16 [4, 1024, 2048], P('dp', 'seq'), may hold values from -0.09375 to 0.09375
- lengths: int32 [4], P('dp'), may hold values from 512 to 1024
- a_query: bfloat16 [5376, 16], replicated, may hold values from -0.078125 to 0.078125
- b_query: bfloat16 [16, 2048], replicated, may hold values from -0.8984375 to 0.8984375
- a_key: bfloat16 [5376, 16], replicated, may hold values from -0.078125 to 0.078125
- b_key: bfloat16 [16, 1024], replicated, may hold values from -0.8984375 to 0.8984375
- a_value: bfloat16 [5376, 16], replicated, may hold values from -0.078125 to 0.078125
- b_value: bfloat16 [16, 1024], replicated, may hold values from -0.8984375 to 0.8984375
Outputs:
- attention: bfloat16 [4, 1024, 2048], P('dp', 'seq')
- grad_a_query: float32 [5376, 16], replicated
- grad_b_query: float32 [16, 2048], replicated
- grad_a_key: float32 [5376, 16], replicated
- grad_b_key: float32 [16, 1024], replicated
- grad_a_value: float32 [5376, 16], replicated
- grad_b_value: float32 [16, 1024], replicated
All inputs are finite; a program needn't handle non-finite values.
Results may differ from a plain program's by a relative error of at most 0.006.
The roundings to bfloat16 on the way count: a program that leaves them out, or rounds other values in their place, can miss the bound.
Values may be sent and summed in bfloat16 or wider, within the bound.
A program may use at most 64 MiB of HBM per device.

v0:
```python
import jax
import jax.numpy as jnp
from jax import lax
from jax.sharding import PartitionSpec as P

HD = 128
WINDOW = 384


attn_scale = 168.0 ** (-0.5)
mask_fill = -1e30


def shifted(value, axis, steps):
    count = lax.axis_size(axis)
    leading, last = (max(0, -steps), min(count, count - steps))
    return lax.ppermute(value, axis, [(source, source + steps) for source in range(leading, last)])


def attend(query, keyset, values, d_out, allowed):
    scores = (
        jnp.einsum("qgrd,kgd->grqk", query, keyset, preferred_element_type=jnp.float32) * attn_scale
    )
    scores = jnp.where(allowed[None, None], scores, mask_fill)
    top_score = jnp.max(scores, axis=-1, keepdims=True)
    raw_weight = jnp.exp(scores - top_score)
    probs = raw_weight / jnp.sum(raw_weight, axis=-1, keepdims=True)
    probs_low = probs.astype(jnp.bfloat16)
    output = jnp.einsum("grqk,kgd->qgrd", probs_low, values, preferred_element_type=jnp.float32)
    dprob = jnp.einsum("qgrd,kgd->grqk", d_out, values, preferred_element_type=jnp.float32)
    delta = jnp.sum(probs * dprob, axis=-1, keepdims=True)
    dscore = (probs * (dprob - delta)).astype(jnp.bfloat16)
    d_query = (
        jnp.einsum("grqk,kgd->qgrd", dscore, keyset, preferred_element_type=jnp.float32)
        * attn_scale
    )
    d_key = (
        jnp.einsum("grqk,qgrd->kgd", dscore, query, preferred_element_type=jnp.float32) * attn_scale
    )
    d_value = jnp.einsum("grqk,qgrd->kgd", probs_low, d_out, preferred_element_type=jnp.float32)
    return (output, d_query, d_key, d_value)


def lifted(base, low, b_matrix):
    return (
        base.astype(jnp.float32) + jnp.dot(low, b_matrix, preferred_element_type=jnp.float32)
    ).astype(jnp.bfloat16)


def fetch_blocks(key_own, value_own, low_pair, hop_count):
    earlier = []
    current = (key_own, value_own, low_pair)
    for hop_index in range(1, hop_count + 1):
        current = shifted((current[0], current[1], current[2]), "seq", 1)
        earlier.append(current)
    return earlier


def shards(
    normed_input,
    q_base,
    k_base,
    v_base,
    d_attn,
    lengths,
    a_query,
    b_query,
    a_key,
    b_key,
    a_value,
    b_value,
):
    rows = normed_input[0]
    tok_rows = rows.shape[0]
    hop_count = (WINDOW + tok_rows - 1) // tok_rows
    rank_size = a_query.shape[1]
    shard_index = lax.axis_index("seq")
    length = lengths[0]
    a_joined = jnp.concatenate([a_query, a_key, a_value], 1)
    low_all = jnp.dot(rows, a_joined, preferred_element_type=jnp.float32).astype(jnp.bfloat16)
    low_query = low_all[:, :rank_size]
    low_pair = low_all[:, rank_size:]
    query = lifted(q_base[0], low_query, b_query)
    key_own = lifted(k_base[0], low_pair[:, :rank_size], b_key)
    value_own = lifted(v_base[0], low_pair[:, rank_size:], b_value)
    earlier = fetch_blocks(key_own, value_own, low_pair, hop_count)
    ordered = list(reversed(earlier))
    key_rows = jnp.concatenate([block[0] for block in ordered] + [key_own], 0)
    value_rows = jnp.concatenate([block[1] for block in ordered] + [value_own], 0)
    low_rows = jnp.concatenate([block[2] for block in ordered] + [low_pair], 0)
    key_span = key_rows.shape[0]
    query_pos = shard_index * tok_rows + jnp.arange(tok_rows, dtype=jnp.int32)
    key_pos = shard_index * tok_rows - hop_count * tok_rows + jnp.arange(key_span, dtype=jnp.int32)
    offset = query_pos[:, None] - key_pos[None, :]
    allowed = (
        (key_pos[None, :] >= 0)
        & (offset >= 0)
        & (offset <= WINDOW)
        & ((key_pos[None, :] < length) | (offset == 0))
    )
    live = query_pos < length
    grad_out = d_attn[0]
    d_out = jnp.where(live[:, None], grad_out, jnp.zeros_like(grad_out))
    groups = key_rows.shape[1] // (2 * HD)
    query_grp = query.reshape(tok_rows, groups, 2, 2, HD).transpose(1, 0, 2, 3, 4)
    dout_grp = d_out.reshape(tok_rows, groups, 2, 2, HD).transpose(1, 0, 2, 3, 4)
    key_grp = key_rows.reshape(key_span, groups, 2, HD).transpose(1, 0, 2, 3)
    value_grp = value_rows.reshape(key_span, groups, 2, HD).transpose(1, 0, 2, 3)

    def per_group(packed):
        return attend(packed[0], packed[1], packed[2], packed[3], allowed)

    out_grp, dquery_grp, dkey_grp, dvalue_grp = lax.map(
        per_group, (query_grp, key_grp, value_grp, dout_grp)
    )
    output = out_grp.transpose(1, 0, 2, 3, 4).reshape(tok_rows, -1)
    attention = jnp.where(live[:, None], output, jnp.zeros_like(output)).astype(jnp.bfloat16)
    d_query = dquery_grp.transpose(1, 0, 2, 3, 4).reshape(tok_rows, -1)
    d_key = dkey_grp.transpose(1, 0, 2, 3).reshape(key_span, -1)
    d_value = dvalue_grp.transpose(1, 0, 2, 3).reshape(key_span, -1)
    highest = lax.Precision.HIGHEST
    u_query = jnp.dot(d_query, b_query.astype(jnp.float32).T, precision=highest).astype(
        jnp.bfloat16
    )
    grad_b_query = jnp.dot(low_query.astype(jnp.float32).T, d_query, precision=highest)
    low_keys = low_rows[:, :rank_size].astype(jnp.float32)
    low_values = low_rows[:, rank_size:].astype(jnp.float32)
    grad_b_key = jnp.dot(low_keys.T, d_key, precision=highest)
    grad_b_value = jnp.dot(low_values.T, d_value, precision=highest)
    ukey_all = jnp.dot(d_key, b_key.astype(jnp.float32).T, precision=highest)
    uvalue_all = jnp.dot(d_value, b_value.astype(jnp.float32).T, precision=highest)
    own_start = hop_count * tok_rows
    ukey_sum = ukey_all[own_start:]
    uvalue_sum = uvalue_all[own_start:]
    for hop_index in range(1, hop_count + 1):
        lower = (hop_count - hop_index) * tok_rows
        came = shifted(
            (ukey_all[lower : lower + tok_rows], uvalue_all[lower : lower + tok_rows]),
            "seq",
            -hop_index,
        )
        ukey_sum = ukey_sum + came[0]
        uvalue_sum = uvalue_sum + came[1]
    u_key = ukey_sum.astype(jnp.bfloat16)
    u_value = uvalue_sum.astype(jnp.bfloat16)
    grad_a_query = jnp.einsum("td,tr->dr", rows, u_query, preferred_element_type=jnp.float32)
    grad_a_key = jnp.einsum("td,tr->dr", rows, u_key, preferred_element_type=jnp.float32)
    grad_a_value = jnp.einsum("td,tr->dr", rows, u_value, preferred_element_type=jnp.float32)
    totals = lax.psum(
        (grad_a_query, grad_b_query, grad_a_key, grad_b_key, grad_a_value, grad_b_value),
        ("seq", "dp"),
    )
    return (attention[None], totals[0], totals[1], totals[2], totals[3], totals[4], totals[5])


def solution(mesh):
    return jax.shard_map(
        shards,
        mesh=mesh,
        in_specs=(
            P("dp", "seq", None),
            P("dp", "seq", None),
            P("dp", "seq", None),
            P("dp", "seq", None),
            P("dp", "seq", None),
            P("dp"),
            P(),
            P(),
            P(),
            P(),
            P(),
            P(),
        ),
        out_specs=(P("dp", "seq", None), P(), P(), P(), P(), P(), P()),
        check_vma=False,
    )
```

profile of v0, /device:TPU:0, one launch (start us, length us, event | category | flops | bytes accessed | tf_op | source)
XLA Modules:
  0.0 273.2 jit_solution(176504505119206906)
XLA Ops:
  8.5 1.6 fusion.82
  10.4 3.1 %collective-permute-start.3 = (bf16[128,1024]{1,0:T(8,128)(2,1)S(1)}, bf16[128,1024]{1,0:T(8,128)(2,1)}, u32[]{:S(2)}, u32[]{:S(2)}) collective-permute-start(bf16[128,1024]{1,0:T(8,128)(2,1)S(1)} %fusion.78), channel_id=1, source_target_pairs={{0,4},{4,8},{8,12},{12,16},{16,20},{20,24},{24,28},{1,5},{5,9},{9,... | collective-permute-start | bytes 786440 | tf_op jit(solution)/shard_map/ppermute | solution.py:17
  13.8 4.5 %collective-permute-start = (bf16[128,1024]{1,0:T(8,128)(2,1)S(1)}, bf16[128,1024]{1,0:T(8,128)(2,1)}, u32[]{:S(2)}, u32[]{:S(2)}) collective-permute-start(bf16[128,1024]{1,0:T(8,128)(2,1)S(1)} %fusion.77), channel_id=1, source_target_pairs={{0,4},{4,8},{8,12},{12,16},{16,20},{20,24},{24,28},{1,5},{5,9},{9,... | collective-permute-start | bytes 786440 | tf_op jit(solution)/shard_map/ppermute | solution.py:17
  18.9 1.9 collective-permute-start.9
  22.1 2.9 %collective-permute-start.4 = (bf16[128,1024]{1,0:T(8,128)(2,1)}, bf16[128,1024]{1,0:T(8,128)(2,1)S(1)}, u32[]{:S(2)}, u32[]{:S(2)}) collective-permute-start(bf16[128,1024]{1,0:T(8,128)(2,1)} %collective-permute-done.3), channel_id=1, source_target_pairs={{0,4},{4,8},{8,12},{12,16},{16,20},{20,24},{24,28},{1,5},{5,9},{9,... | collective-permute-start | bytes 786440 | tf_op jit(solution)/shard_map/ppermute | solution.py:17
  25.0 2.6 collective-permute-start.1
  28.5 2.8 %collective-permute-start.10 = (bf16[128,32]{0,1:T(8,128)(2,1)}, bf16[128,32]{0,1:T(8,128)(2,1)S(1)}, u32[]{:S(2)}, u32[]{:S(2)}) collective-permute-start(bf16[128,32]{0,1:T(8,128)(2,1)} %collective-permute-done.9), channel_id=1, source_target_pairs={{0,4},{4,8},{8,12},{12,16},{16,20},{20,24},{24,28},{1,5},{5,9},{9,... | collective-permute-start | bytes 24584 | tf_op jit(solution)/shard_map/ppermute | solution.py:17
  31.3 1.9 collective-permute-start.5
  33.3 1.9 collective-permute-start.11
  35.2 3.9 %collective-permute-start.2 = (bf16[128,1024]{1,0:T(8,128)(2,1)}, bf16[128,1024]{1,0:T(8,128)(2,1)}, u32[]{:S(2)}, u32[]{:S(2)}) collective-permute-start(bf16[128,1024]{1,0:T(8,128)(2,1)} %collective-permute-done.1), channel_id=1, source_target_pairs={{0,4},{4,8},{8,12},{12,16},{16,20},{20,24},{24,28},{1,5},{5,9},{9,... | collective-permute-start | bytes 786440 | tf_op jit(solution)/shard_map/ppermute | solution.py:17
  41.0 1.3 pad_maximum_fusion.2
  46.2 1.3 copy.57
  47.6 47.8 %while.17 = (s32[]{:T(128)}, bf16[4,128,2,2,128]{1,4,3,2,0:T(8,128)(2,1)}, f32[4,128,2,2,128]{1,4,3,2,0:T(8,128)}, f32[4,512,2,128]{1,3,2,0:T(8,128)}, f32[4,512...) while((s32[]{:T(128)}, ...), condition=%wide.region_4.5_spmd.clone, body=%wide.region_0.4_spmd.clone.sunk | while | flops 543098880 | bytes 17327832 | solution.py:113
  48.5 1.4 fusion.169
  49.9 1.3 multiply_reduce_fusion.2
  51.4 2.1 fusion.172
  54.5 2.5 fusion.173
  57.0 1.7 fusion.170
  60.4 1.4 fusion.169
  61.9 1.3 multiply_reduce_fusion.2
  63.4 2.1 fusion.172
  66.5 2.5 fusion.173
  69.0 1.7 fusion.170
  72.4 1.4 fusion.169
  73.8 1.4 multiply_reduce_fusion.2
  75.3 2.1 fusion.172
  78.4 2.5 fusion.173
  80.9 1.7 fusion.170
  84.3 1.4 fusion.169
  85.8 1.4 multiply_reduce_fusion.2
  87.3 2.1 fusion.172
  90.3 2.5 fusion.173
  92.8 1.7 fusion.170
  95.3 2.5 fusion.118
  98.7 1.7 fusion.90
  100.4 1.7 fusion.92
  103.4 1.3 collective-permute-start.13
  104.7 1.3 collective-permute-start.14
  109.4 1.9 fusion.104
  112.6 1.4 collective-permute-start.8
  115.1 3.3 %collective-permute-done.7 = f32[128,16]{0,1:T(8,128)S(1)} collective-permute-done((f32[128,16]{0,1:T(8,128)S(1)}, f32[128,16]{0,1:T(8,128)S(1)}, u32[]{:S(2)}, u32[]{:S(2)}) %collective-permute-start.7) | collective-permute-done | bytes 8224 | tf_op jit(solution)/shard_map/ppermute | solution.py:17
  118.5 2.5 collective-permute-done.8
  123.2 134.2 %all-reduce.3.cloned.1.call-done = (f32[5376,16]{0,1:T(8,128)}, f32[16,2048]{1,0:T(8,128)}, f32[5376,16]{0,1:T(8,128)}, f32[16,1024]{1,0:T(8,128)}, f32[5376,16]{0,1:T(8,128)}, /*index=5*/f32[16,1024]{1,0:T(8,128)}) async-done(((f32[5376,16]{0,1:T(8,128)}, f32[16,2048]{1,0:T(8,128)}, f32[5376,16]{0,1:T(8,128)}, f32[16,1024]{1,0:T(8,128)}, f32[5376,16]{0,1:T(8,128)}, /*index=5*/f32[16,1024]{1,0:T(8,128)}), ...) | async-done | bytes 1294352 | tf_op jit(solution)/shard_map/psum | solution.py:149
  257.5 1.8 copy.96
  259.2 1.6 copy.97
  260.8 1.7 copy.98
  262.5 1.5 copy.99
  264.0 1.7 copy.100
  (126 shorter events, 31.7 us)
Async XLA Ops:
  7.2 1.3 copy-start
  7.2 3.0 %copy-start.14 = (bf16[1,128,1024]{2,1,0:T(8,128)(2,1)S(1)}, bf16[1,128,1024]{2,1,0:T(8,128)(2,1)}, u32[]{:S(2)}) copy-start(bf16[1,128,1024]{2,1,0:T(8,128)(2,1)} %param.16) | copy-start | bytes 786436
  7.2 3.0 %copy-start.17 = (bf16[16,1024]{1,0:T(8,128)(2,1)S(1)}, bf16[16,1024]{1,0:T(8,128)(2,1)}, u32[]{:S(2)}) copy-start(bf16[16,1024]{1,0:T(8,128)(2,1)} %param.23) | copy-start | bytes 98308
  7.2 6.3 %copy-start.15 = (bf16[1,128,1024]{2,1,0:T(8,128)(2,1)S(1)}, bf16[1,128,1024]{2,1,0:T(8,128)(2,1)}, u32[]{:S(2)}) copy-start(bf16[1,128,1024]{2,1,0:T(8,128)(2,1)} %param.17) | copy-start | bytes 786436
  7.2 14.2 %copy-start.7 = (bf16[1,128,2048]{2,1,0:T(8,128)(2,1)S(1)}, bf16[1,128,2048]{2,1,0:T(8,128)(2,1)}, u32[]{:S(2)}) copy-start(bf16[1,128,2048]{2,1,0:T(8,128)(2,1)} %param.18) | copy-start | bytes 1572868
  7.2 14.5 %copy-start.8 = (bf16[1,128,2048]{2,1,0:T(8,128)(2,1)S(1)}, bf16[1,128,2048]{2,1,0:T(8,128)(2,1)}, u32[]{:S(2)}) copy-start(bf16[1,128,2048]{2,1,0:T(8,128)(2,1)} %param.15) | copy-start | bytes 1572868
  7.2 14.5 %copy-start.12 = (bf16[16,2048]{1,0:T(8,128)(2,1)S(1)}, bf16[16,2048]{1,0:T(8,128)(2,1)}, u32[]{:S(2)}) copy-start(bf16[16,2048]{1,0:T(8,128)(2,1)} %param.21) | copy-start | bytes 196612
  7.2 250.2 %all-reduce.3.cloned.1.call-start = ((), (), s32[]{:S(2)}) async-start(), calls=%async_computation | async-start | bytes 2588672 | tf_op jit(solution)/shard_map/psum | solution.py:149
  8.5 5.0 %copy-start.16 = (bf16[16,1024]{1,0:T(8,128)(2,1)S(1)}, bf16[16,1024]{1,0:T(8,128)(2,1)}, u32[]{:S(2)}) copy-start(bf16[16,1024]{1,0:T(8,128)(2,1)} %param.25) | copy-start | bytes 98308
  10.2 18.3 %copy-start.21 = (bf16[128,48]{0,1:T(8,128)(2,1)}, bf16[128,48]{0,1:T(8,128)(2,1)S(1)}, u32[]{:S(2)}) copy-start(bf16[128,48]{0,1:T(8,128)(2,1)S(1)} %fusion.82) | copy-start | bytes 36868
  10.4 11.6 %collective-permute-start.3 = (bf16[128,1024]{1,0:T(8,128)(2,1)S(1)}, bf16[128,1024]{1,0:T(8,128)(2,1)}, u32[]{:S(2)}, u32[]{:S(2)}) collective-permute-start(bf16[128,1024]{1,0:T(8,128)(2,1)S(1)} %fusion.78), channel_id=1, source_target_pairs={{0,4},{4,8},{8,12},{12,16},{16,20},{20,24},{24,28},{1,5},{5,9},{9,... | collective-permute-start | bytes 786440 | tf_op jit(solution)/shard_map/ppermute | solution.py:17
  13.8 26.2 %copy-start.5 = (bf16[128,1024]{1,0:T(8,128)(2,1)}, bf16[128,1024]{1,0:T(8,128)(2,1)S(1)}, u32[]{:S(2)}) copy-start(bf16[128,1024]{1,0:T(8,128)(2,1)S(1)} %fusion.77) | copy-start | bytes 786436
  13.8 11.2 %collective-permute-start = (bf16[128,1024]{1,0:T(8,128)(2,1)S(1)}, bf16[128,1024]{1,0:T(8,128)(2,1)}, u32[]{:S(2)}, u32[]{:S(2)}) collective-permute-start(bf16[128,1024]{1,0:T(8,128)(2,1)S(1)} %fusion.77), channel_id=1, source_target_pairs={{0,4},{4,8},{8,12},{12,16},{16,20},{20,24},{24,28},{1,5},{5,9},{9,... | collective-permute-start | bytes 786440 | tf_op jit(solution)/shard_map/ppermute | solution.py:17
  18.9 9.6 %collective-permute-start.9 = (bf16[128,32]{0,1:T(8,128)(2,1)}, bf16[128,32]{0,1:T(8,128)(2,1)}, u32[]{:S(2)}, u32[]{:S(2)}) collective-permute-start(bf16[128,32]{0,1:T(8,128)(2,1)} %slice.65), channel_id=1, source_target_pairs={{0,4},{4,8},{8,12},{12,16},{16,20},{20,24},{24,28},{1,5},{5,9},{9,... | collective-permute-start | bytes 24584 | tf_op jit(solution)/shard_map/ppermute | solution.py:17
  21.5 11.8 %copy-start.22 = (pred[128]{0:T(512)(128)(4,1)}, pred[128]{0:T(512)(128)(4,1)S(1)}, u32[]{:S(2)}) copy-start(pred[128]{0:T(512)(128)(4,1)S(1)} %broadcast_compare_fusion) | copy-start | bytes 388
  22.1 9.2 %collective-permute-start.4 = (bf16[128,1024]{1,0:T(8,128)(2,1)}, bf16[128,1024]{1,0:T(8,128)(2,1)S(1)}, u32[]{:S(2)}, u32[]{:S(2)}) collective-permute-start(bf16[128,1024]{1,0:T(8,128)(2,1)} %collective-permute-done.3), channel_id=1, source_target_pairs={{0,4},{4,8},{8,12},{12,16},{16,20},{20,24},{24,28},{1,5},{5,9},{9,... | collective-permute-start | bytes 786440 | tf_op jit(solution)/shard_map/ppermute | solution.py:17
  25.0 10.2 %collective-permute-start.1 = (bf16[128,1024]{1,0:T(8,128)(2,1)}, bf16[128,1024]{1,0:T(8,128)(2,1)}, u32[]{:S(2)}, u32[]{:S(2)}) collective-permute-start(bf16[128,1024]{1,0:T(8,128)(2,1)} %collective-permute-done), channel_id=1, source_target_pairs={{0,4},{4,8},{8,12},{12,16},{16,20},{20,24},{24,28},{1,5},{5,9},{9,... | collective-permute-start | bytes 786440 | tf_op jit(solution)/shard_map/ppermute | solution.py:17
  28.5 4.8 %collective-permute-start.10 = (bf16[128,32]{0,1:T(8,128)(2,1)}, bf16[128,32]{0,1:T(8,128)(2,1)S(1)}, u32[]{:S(2)}, u32[]{:S(2)}) collective-permute-start(bf16[128,32]{0,1:T(8,128)(2,1)} %collective-permute-done.9), channel_id=1, source_target_pairs={{0,4},{4,8},{8,12},{12,16},{16,20},{20,24},{24,28},{1,5},{5,9},{9,... | collective-permute-start | bytes 24584 | tf_op jit(solution)/shard_map/ppermute | solution.py:17
  31.3 11.0 %collective-permute-start.5 = (bf16[128,1024]{1,0:T(8,128)(2,1)S(1)}, bf16[128,1024]{1,0:T(8,128)(2,1)S(1)}, u32[]{:S(2)}, u32[]{:S(2)}) collective-permute-start(bf16[128,1024]{1,0:T(8,128)(2,1)S(1)} %collective-permute-done.4), channel_id=1, source_target_pairs={{0,4},{4,8},{8,12},{12,16},{16,20},{20,24},{24,28},{1,5},{5,9},{9,... | collective-permute-start | bytes 786440 | tf_op jit(solution)/shard_map/ppermute | solution.py:17
  33.3 7.7 %collective-permute-start.11 = (bf16[128,32]{0,1:T(8,128)(2,1)S(1)}, bf16[128,32]{0,1:T(8,128)(2,1)S(1)}, u32[]{:S(2)}, u32[]{:S(2)}) collective-permute-start(bf16[128,32]{0,1:T(8,128)(2,1)S(1)} %collective-permute-done.10), channel_id=1, source_target_pairs={{0,4},{4,8},{8,12},{12,16},{16,20},{20,24},{24,28},{1,5},{5,9},{9,... | collective-permute-start | bytes 24584 | tf_op jit(solution)/shard_map/ppermute | solution.py:17
  35.2 9.0 %collective-permute-start.2 = (bf16[128,1024]{1,0:T(8,128)(2,1)}, bf16[128,1024]{1,0:T(8,128)(2,1)}, u32[]{:S(2)}, u32[]{:S(2)}) collective-permute-start(bf16[128,1024]{1,0:T(8,128)(2,1)} %collective-permute-done.1), channel_id=1, source_target_pairs={{0,4},{4,8},{8,12},{12,16},{16,20},{20,24},{24,28},{1,5},{5,9},{9,... | collective-permute-start | bytes 786440 | tf_op jit(solution)/shard_map/ppermute | solution.py:17
  44.1 1.0 copy-start.6
  51.4 3.1 %copy-start.4 = (bf16[4,128,2,2,128]{4,1,3,2,0:T(8,128)(2,1)S(1)}, bf16[4,128,2,2,128]{4,1,3,2,0:T(8,128)(2,1)}, u32[]{:S(2)}) copy-start(bf16[4,128,2,2,128]{4,1,3,2,0:T(8,128)(2,1)} %get-tuple-element.277) | copy-start | bytes 1572868 | tf_op jit(solution)/shard_map/while
  54.5 2.5 copy-start.9
  58.7 0.8 copy-start.10
  63.4 3.1 %copy-start.4 = (bf16[4,128,2,2,128]{4,1,3,2,0:T(8,128)(2,1)S(1)}, bf16[4,128,2,2,128]{4,1,3,2,0:T(8,128)(2,1)}, u32[]{:S(2)}) copy-start(bf16[4,128,2,2,128]{4,1,3,2,0:T(8,128)(2,1)} %get-tuple-element.277) | copy-start | bytes 1572868 | tf_op jit(solution)/shard_map/while
  66.5 2.5 copy-start.9
  70.7 0.8 copy-start.10
  75.3 3.1 %copy-start.4 = (bf16[4,128,2,2,128]{4,1,3,2,0:T(8,128)(2,1)S(1)}, bf16[4,128,2,2,128]{4,1,3,2,0:T(8,128)(2,1)}, u32[]{:S(2)}) copy-start(bf16[4,128,2,2,128]{4,1,3,2,0:T(8,128)(2,1)} %get-tuple-element.277) | copy-start | bytes 1572868 | tf_op jit(solution)/shard_map/while
  78.4 2.5 copy-start.9
  87.3 3.1 %copy-start.4 = (bf16[4,128,2,2,128]{4,1,3,2,0:T(8,128)(2,1)S(1)}, bf16[4,128,2,2,128]{4,1,3,2,0:T(8,128)(2,1)}, u32[]{:S(2)}) copy-start(bf16[4,128,2,2,128]{4,1,3,2,0:T(8,128)(2,1)} %get-tuple-element.277) | copy-start | bytes 1572868 | tf_op jit(solution)/shard_map/while
  90.3 2.5 copy-start.9
  94.5 0.8 copy-start.10
  95.3 2.5 copy-start.1
  95.3 2.5 copy-start.18
  95.3 3.3 %copy-start.2 = (f32[4,512,2,128]{1,3,2,0:T(8,128)S(1)}, f32[4,512,2,128]{1,3,2,0:T(8,128)}, u32[]{:S(2)}) copy-start(f32[4,512,2,128]{1,3,2,0:T(8,128)} %get-tuple-element.65) | copy-start | bytes 6291460
  95.3 3.3 %copy-start.19 = (bf16[512,32]{0,1:T(8,128)(2,1)S(1)}, bf16[512,32]{0,1:T(8,128)(2,1)}, u32[]{:S(2)}) copy-start(bf16[512,32]{0,1:T(8,128)(2,1)} %pad_maximum_fusion.2) | copy-start | bytes 98308
  98.7 8.6 %copy-start.3 = (f32[4,128,2,2,128]{1,4,3,2,0:T(8,128)S(1)}, f32[4,128,2,2,128]{1,4,3,2,0:T(8,128)}, u32[]{:S(2)}) copy-start(f32[4,128,2,2,128]{1,4,3,2,0:T(8,128)} %get-tuple-element.63) | copy-start | bytes 3145732
  98.7 8.6 %copy-start.13 = (bf16[16,2048]{1,0:T(8,128)(2,1)S(1)}, bf16[16,2048]{1,0:T(8,128)(2,1)}, u32[]{:S(2)}) copy-start(bf16[16,2048]{1,0:T(8,128)(2,1)} %param.21) | copy-start | bytes 196612
  102.1 10.5 %collective-permute-start.12 = (f32[128,16]{0,1:T(8,128)S(1)}, f32[128,16]{0,1:T(8,128)S(1)}, u32[]{:S(2)}, u32[]{:S(2)}) collective-permute-start(f32[128,16]{0,1:T(8,128)S(1)} %get-tuple-element.147), channel_id=1, source_target_pairs={{4,0},{8,4},{12,8},{16,12},{20,16},{24,20},{28,24},{5,1},{9,5},{13... | collective-permute-start | bytes 24584 | tf_op jit(solution)/shard_map/ppermute | solution.py:17
  103.4 10.7 %collective-permute-start.13 = (f32[128,16]{0,1:T(8,128)S(1)}, f32[128,16]{0,1:T(8,128)S(1)}, u32[]{:S(2)}, u32[]{:S(2)}) collective-permute-start(f32[128,16]{0,1:T(8,128)S(1)} %get-tuple-element.149), channel_id=1, source_target_pairs={{8,0},{12,4},{16,8},{20,12},{24,16},{28,20},{9,1},{13,5},{17,9},{2... | collective-permute-start | bytes 24584 | tf_op jit(solution)/shard_map/ppermute | solution.py:17
  104.7 9.4 %collective-permute-start.14 = (f32[128,16]{0,1:T(8,128)S(1)}, f32[128,16]{0,1:T(8,128)S(1)}, u32[]{:S(2)}, u32[]{:S(2)}) collective-permute-start(f32[128,16]{0,1:T(8,128)S(1)} %get-tuple-element.148), channel_id=1, source_target_pairs={{12,0},{16,4},{20,8},{24,12},{28,16},{13,1},{17,5},{21,9},{25,13},... | collective-permute-start | bytes 24584 | tf_op jit(solution)/shard_map/ppermute | solution.py:17
  106.0 9.1 %collective-permute-start.6 = (f32[128,16]{0,1:T(8,128)S(1)}, f32[128,16]{0,1:T(8,128)S(1)}, u32[]{:S(2)}, u32[]{:S(2)}) collective-permute-start(f32[128,16]{0,1:T(8,128)S(1)} %get-tuple-element.150), channel_id=1, source_target_pairs={{4,0},{8,4},{12,8},{16,12},{20,16},{24,20},{28,24},{5,1},{9,5},{13... | collective-permute-start | bytes 24584 | tf_op jit(solution)/shard_map/ppermute | solution.py:17
  111.3 7.2 %collective-permute-start.7 = (f32[128,16]{0,1:T(8,128)S(1)}, f32[128,16]{0,1:T(8,128)S(1)}, u32[]{:S(2)}, u32[]{:S(2)}) collective-permute-start(f32[128,16]{0,1:T(8,128)S(1)} %get-tuple-element.152), channel_id=1, source_target_pairs={{8,0},{12,4},{16,8},{20,12},{24,16},{28,20},{9,1},{13,5},{17,9},{2... | collective-permute-start | bytes 24584 | tf_op jit(solution)/shard_map/ppermute | solution.py:17
  112.6 9.4 %copy-start.11 = (bf16[4,128,2,2,128]{1,4,3,2,0:T(8,128)(2,1)S(1)}, bf16[4,128,2,2,128]{1,4,3,2,0:T(8,128)(2,1)}, u32[]{:S(2)}) copy-start(bf16[4,128,2,2,128]{1,4,3,2,0:T(8,128)(2,1)} %get-tuple-element.62) | copy-start | bytes 1572868
  112.6 8.3 %collective-permute-start.8 = (f32[128,16]{0,1:T(8,128)S(1)}, f32[128,16]{0,1:T(8,128)S(1)}, u32[]{:S(2)}, u32[]{:S(2)}) collective-permute-start(f32[128,16]{0,1:T(8,128)S(1)} %get-tuple-element.151), channel_id=1, source_target_pairs={{12,0},{16,4},{20,8},{24,12},{28,16},{13,1},{17,5},{21,9},{25,13},... | collective-permute-start | bytes 24584 | tf_op jit(solution)/shard_map/ppermute | solution.py:17
  115.1 7.1 %copy-start.23 = (pred[128]{0:T(512)(128)(4,1)S(1)}, pred[128]{0:T(512)(128)(4,1)}, u32[]{:S(2)}) copy-start(pred[128]{0:T(512)(128)(4,1)} %copy-done.22) | copy-start | bytes 388
  257.5 8.3 %copy-start.20 = (f32[16,1024]{1,0:T(8,128)S(1)}, f32[16,1024]{1,0:T(8,128)}, u32[]{:S(2)}) copy-start(f32[16,1024]{1,0:T(8,128)} %get-tuple-element.290) | copy-start | bytes 196612
  (1 other events, 0.8 us)
Sparse Core Ops, SparseCore 0:
  122.2 135.2 all-reduce.2
where the time goes:
time: 275 us; the launch traced here: 273 us
  waiting for transfers between devices  140 us (51%)
  matrix products  55.3 us (20%)
  starting transfers between devices  33.4 us (12%)
  local copies, waits for them, and re-layouts  18.8 us (7%)
  between operations  15.2 us (6%)
  other arithmetic  10.2 us (4%)
    psum x1, waiting for transfers between devices, shards(): lax.psum((grad_a_query, grad_b_query, grad_a_key, grad_b_key, grad_a_valu...  134 us
    ppermute x15, starting transfers between devices, shifted(): lax.ppermute(value, axis, [(source, source + steps) for source in range(l...  33.4 us
    unnamed x49, local copies, waits for them, and re-layouts  11.3 us
    dot_general x4, matrix products, attend(): jnp.einsum('grqk,qgrd->kgd', probs_low, d_out, preferred_element_type=jnp...  10 us
    dot_general x4, matrix products, attend(): jnp.einsum('grqk,qgrd->kgd', dscore, query, preferred_element_type=jnp.fl...  8.35 us
    dot_general x4, matrix products, attend(): jnp.einsum('grqk,kgd->qgrd', probs_low, values, preferred_element_type=jn...  6.73 us
    ppermute x15, waiting for transfers between devices, shifted(): lax.ppermute(value, axis, [(source, source + steps) for source in range(l...  5.89 us
    sub x4, matrix products, attend(): raw_weight = jnp.exp(scores - top_score)  5.62 us
  transfers between devices with their start and end apart: 16, of which 3 were waited for; matrix products, arithmetic and copies ran while one was open for 5% of the time, Pallas kernels for 0%

commit v1 on v0

v1 whole, which is shorter than its diff:
```python
import functools

import jax
import jax.numpy as jnp
from jax import lax
from jax.experimental import pallas as pl
from jax.experimental.pallas import tpu as pltpu
from jax.sharding import PartitionSpec as P

HD = 128
WINDOW = 384
HOPS = 3
LANES = 128

attn_scale = 168.0 ** (-0.5)
mask_fill = -1e30
f32 = jnp.float32
bf16 = jnp.bfloat16


def dot(left, right, left_dim, right_dim):
    return lax.dot_general(
        left, right, (((left_dim,), (right_dim,)), ((), ())), preferred_element_type=f32
    )


def halves(value):
    high = value.astype(bf16)
    return high, (value - high.astype(f32)).astype(bf16)


def remote(src, dst, send_sem, recv_sem, **device):
    return pltpu.make_async_remote_copy(
        src_ref=src,
        dst_ref=dst,
        send_sem=send_sem,
        recv_sem=recv_sem,
        device_id=device,
        device_id_type=pl.DeviceIdType.MESH,
    )


def kernel(
    n_seq,
    n_dp,
    per_piece,
    rows,
    q_base,
    k_base,
    v_base,
    d_attn,
    length_ref,
    a_query,
    a_key,
    a_value,
    b_query,
    b_key,
    b_value,
    attention,
    out_aq,
    out_bq,
    out_ak,
    out_bk,
    out_av,
    out_bv,
    qs,
    ds,
    kv,
    lows,
    bias,
    b2q,
    b2k,
    b2v,
    uq,
    ukv,
    u_came,
    gsum,
    core_in,
    chip_out,
    chip_in,
    dp_out,
    dp_in,
    final,
    kv_send,
    kv_recv,
    relay_send,
    low_send,
    low_recv,
    u_send,
    u_recv,
    s1_send,
    s1_recv,
    s2_send,
    s2_recv,
    s3_send,
    s3_recv,
    s4_send,
    s4_recv,
    s5_send,
    s5_recv,
    s6_send,
    s6_recv,
):
    tok = rows.shape[0]
    width = rows.shape[1]
    rank = b_query.shape[0]
    groups = k_base.shape[1] // HD
    chunks = groups // 2
    n_chip = n_seq // 2
    seq = lax.axis_index("seq")
    dp = lax.axis_index("dp")
    core = lax.rem(seq, 2)
    chip = seq // 2
    sibling = seq + 1 - 2 * core
    own = HOPS * tok
    span = own + tok

    barrier = pltpu.get_barrier_semaphore()
    offsets = {step % n_seq for hop in range(1, HOPS + 1) for step in (hop, -hop)}
    offsets |= set(range(2, n_seq, 2))
    offsets.discard(0)
    for offset in sorted(offsets):
        pl.semaphore_signal(
            barrier,
            inc=1,
            device_id={"seq": lax.rem(seq + offset, n_seq)},
            device_id_type=pl.DeviceIdType.MESH,
        )
    for offset in range(1, n_dp):
        pl.semaphore_signal(
            barrier,
            inc=1,
            device_id={"dp": lax.rem(dp + offset, n_dp)},
            device_id_type=pl.DeviceIdType.MESH,
        )

    joined = jnp.concatenate(
        [a_query[...], a_key[...], a_value[...], jnp.zeros((LANES - 3 * rank, width), bf16)], 0
    )
    low = dot(rows[...], joined, 1, 1)
    low_t = jnp.transpose(low.astype(bf16).astype(f32)).astype(bf16)
    lowq_t = low_t[:rank]
    lowk_t = low_t[rank : 2 * rank]
    lowv_t = low_t[2 * rank : 3 * rank]
    lows[HOPS] = low_t[rank : 3 * rank]
    for chunk in range(chunks):
        cols = slice(chunk * 2 * HD, (chunk + 1) * 2 * HD)
        kv[chunk, own:span, : 2 * HD] = (
            k_base[:, cols].astype(f32) + dot(lowk_t, b_key[:, cols], 0, 0)
        ).astype(bf16)
        kv[chunk, own:span, 2 * HD :] = (
            v_base[:, cols].astype(f32) + dot(lowv_t, b_value[:, cols], 0, 0)
        ).astype(bf16)

    for hop in range(1, HOPS + 1):
        @pl.when(seq < hop)
        def _():
            start = (HOPS - hop) * tok
            for chunk in range(chunks):
                kv[chunk, start : start + tok, :] = jnp.zeros((tok, 4 * HD), bf16)
            lows[HOPS - hop] = jnp.zeros(lows.shape[1:], bf16)

        @pl.when(seq + hop >= n_seq)
        def _():
            u_came[hop - 1] = jnp.zeros(u_came.shape[1:], f32)

    pl.semaphore_wait(barrier, len(offsets) + n_dp - 1)

    def slot(chunk, hop):
        start = (HOPS - hop) * tok
        if not isinstance(start, int):
            start = pl.multiple_of(start, tok)
        return kv.at[chunk, pl.ds(start, tok), :]

    near_hop = 1 + 2 * core
    relay_hop = 3 - 2 * core

    def send_two(chunk):
        return remote(
            slot(chunk, 0), slot(chunk, 2), kv_send.at[chunk, 0], kv_recv.at[chunk, 1],
            seq=lax.rem(seq + 2, n_seq),
        )

    def send_near(chunk):
        return remote(
            slot(chunk, 0), slot(chunk, near_hop), kv_send.at[chunk, 1],
            kv_recv.at[chunk, near_hop - 1], seq=lax.rem(seq + near_hop, n_seq),
        )

    def relay(chunk):
        return remote(
            slot(chunk, 2), slot(chunk, relay_hop), relay_send.at[chunk],
            kv_recv.at[chunk, relay_hop - 1], seq=sibling,
        )

    def arrival(chunk, hop):
        return remote(
            slot(chunk, 0), slot(chunk, hop), relay_send.at[chunk], kv_recv.at[chunk, hop - 1],
            seq=sibling,
        )

    def send_low(hop):
        return remote(
            lows.at[HOPS], lows.at[HOPS - hop], low_send.at[hop - 1], low_recv.at[hop - 1],
            seq=lax.rem(seq + hop, n_seq),
        )

    def send_u(hop):
        return remote(
            ukv.at[HOPS - hop], u_came.at[hop - 1], u_send.at[hop - 1], u_recv.at[hop - 1],
            seq=lax.rem(seq - hop + n_seq, n_seq),
        )

    for chunk in range(chunks):
        @pl.when(seq + 2 < n_seq)
        def _():
            send_two(chunk).start()

        @pl.when(seq + near_hop < n_seq)
        def _():
            send_near(chunk).start()

        if chunk == 0:
            for hop in range(1, HOPS + 1):
                @pl.when(seq + hop < n_seq)
                def _():
                    send_low(hop).start()

    length = length_ref[0]
    place = seq * tok + lax.broadcasted_iota(jnp.int32, (tok, 1), 0)
    live = place < length
    for group in range(groups):
        cols = slice(group * 2 * HD, (group + 1) * 2 * HD)
        query = (q_base[:, cols].astype(f32) + dot(lowq_t, b_query[:, cols], 0, 0)).astype(bf16)
        grad = jnp.where(live, d_attn[:, cols].astype(f32), 0.0).astype(bf16)
        for side in range(2):
            part = slice(side * HD, (side + 1) * HD)
            qs[group, side * tok : (side + 1) * tok, :] = query[:, part]
            ds[group, side * tok : (side + 1) * tok, :] = grad[:, part]
            at = slice((2 * group + side) * HD, (2 * group + side + 1) * HD)
            b2q[2 * group + side, :, :HD] = b_query[:, at]
            b2q[2 * group + side, :, HD:] = b_query[:, at]
        at = slice(group * HD, (group + 1) * HD)
        for twice, single in ((b2k, b_key), (b2v, b_value)):
            twice[group, :, :HD] = single[:, at]
            twice[group, :, HD:] = single[:, at]
    key_place = (seq - HOPS) * tok + lax.broadcasted_iota(jnp.int32, (tok, span), 1)
    query_place = seq * tok + lax.broadcasted_iota(jnp.int32, (tok, span), 0)
    distance = query_place - key_place
    allowed = (
        (key_place >= 0)
        & (distance >= 0)
        & (distance <= WINDOW)
        & ((key_place < length) | (distance == 0))
    )
    bias[...] = jnp.where(allowed, 0.0, mask_fill)
    uq[...] = jnp.zeros_like(uq)
    ukv[...] = jnp.zeros_like(ukv)

    tiles_a = width // LANES
    heads = 2 * groups
    at_bq = 3 * tiles_a
    at_bk = at_bq + heads
    at_bv = at_bk + groups
    tiles = at_bv + groups
    if tiles < gsum.shape[0]:
        gsum[tiles:] = jnp.zeros((gsum.shape[0] - tiles, rank, LANES), f32)

    for hop in range(1, HOPS + 1):
        @pl.when(seq >= hop)
        def _():
            remote(
                lows.at[HOPS], lows.at[HOPS - hop], low_send.at[hop - 1], low_recv.at[hop - 1],
                seq=sibling,
            ).wait_recv()
    low_span = jnp.concatenate([lows[index] for index in range(HOPS + 1)], 1)
    lowk2 = jnp.concatenate([low_span[:rank], low_span[:rank]], 1)
    lowv2 = jnp.concatenate([low_span[rank:], low_span[rank:]], 1)
    lowq2 = jnp.concatenate([lowq_t, lowq_t], 1)

    def head(chunk, side):
        group = 2 * chunk + side
        keys = kv[chunk, :, side * HD : (side + 1) * HD]
        values = kv[chunk, :, (2 + side) * HD : (3 + side) * HD]
        query = qs[group]
        d_out = ds[group]
        scores = dot(query, keys, 1, 1) * attn_scale
        scores = (scores.reshape(2, tok, span) + bias[...][None]).reshape(2 * tok, span)
        top = jnp.max(scores, axis=-1, keepdims=True)
        raw = jnp.exp(scores - top)
        probs = raw * (1.0 / jnp.sum(raw, axis=-1, keepdims=True))
        probs_low = probs.astype(bf16)
        output = dot(probs_low, values, 1, 0)
        dprob = dot(d_out, values, 1, 1)
        delta = jnp.sum(probs * dprob, axis=-1, keepdims=True)
        dscore = (probs * (dprob - delta)).astype(bf16)
        d_query = dot(dscore, keys, 1, 0) * attn_scale
        d_key = dot(query, dscore, 0, 0) * attn_scale
        d_value = dot(d_out, probs_low, 0, 0)
        for grad, low2, twice, at, base in (
            (d_key, lowk2, b2k, at_bk, 0),
            (d_value, lowv2, b2v, at_bv, rank),
        ):
            high, rest = halves(grad)
            up = dot(twice[group], jnp.concatenate([high, rest], 0), 1, 0)
            for index in range(HOPS + 1):
                ukv[index, base : base + rank, :] += up[:, index * tok : (index + 1) * tok]
            gsum[at + group] = dot(low2, jnp.concatenate([high, rest], 1), 1, 1)
        high, rest = halves(d_query)
        total = uq[...]
        for part in range(2):
            at = slice(part * tok, (part + 1) * tok)
            number = 2 * group + part
            total += dot(b2q[number], jnp.concatenate([high[at], rest[at]], 1), 1, 1)
            gsum[at_bq + number] = dot(lowq2, jnp.concatenate([high[at], rest[at]], 0), 1, 0)
            kept = jnp.where(live, output[at], 0.0).astype(bf16)
            attention[:, pl.ds(pl.multiple_of(number * HD, HD), HD)] = kept
        uq[...] = total

    @pl.when(chip >= 1)
    def _():
        arrival(0, 2).wait_recv()
        relay(0).start()

    def step(chunk, carry):
        for hop in (1, 3):
            @pl.when(seq >= hop)
            def _():
                arrival(chunk, hop).wait_recv()

        head(chunk, 0)

        @pl.when((chip >= 1) & (chunk + 1 < chunks))
        def _():
            later = lax.rem(chunk + 1, chunks)
            arrival(later, 2).wait_recv()
            relay(later).start()

        head(chunk, 1)
        return carry

    lax.fori_loop(0, chunks, step, 0)

    for hop in range(1, HOPS + 1):
        @pl.when(seq >= hop)
        def _():
            send_u(hop).start()

    grad = dot(uq[...].astype(bf16), rows[...], 1, 0)
    for tile in range(tiles_a):
        gsum[tile] = grad[:, tile * LANES : (tile + 1) * LANES]
    for hop in range(1, HOPS + 1):
        @pl.when(seq + hop < n_seq)
        def _():
            remote(
                ukv.at[HOPS - hop], u_came.at[hop - 1], u_send.at[hop - 1], u_recv.at[hop - 1],
                seq=sibling,
            ).wait_recv()
    pair = ukv[HOPS] + u_came[0] + u_came[1] + u_came[2]
    grad = dot(pair.astype(bf16), rows[...], 1, 0)
    for tile in range(tiles_a):
        at = slice(tile * LANES, (tile + 1) * LANES)
        gsum[tiles_a + tile] = grad[:rank, at]
        gsum[2 * tiles_a + tile] = grad[rank:, at]

    per_chip = n_dp * per_piece
    half = n_chip * per_chip

    def ordered(index):
        return lax.rem(chip + index, n_chip)

    def core_copy(index):
        at = ordered(index) * per_chip
        return remote(
            gsum.at[pl.ds((1 - core) * half + at, per_chip)],
            core_in.at[pl.ds(at, per_chip)],
            s1_send.at[index], s1_recv.at[index], seq=sibling,
        )

    def chip_copy(index):
        return remote(
            chip_out.at[index - 1], chip_in.at[index - 1], s2_send.at[index - 1],
            s2_recv.at[index - 1], seq=2 * ordered(index) + core,
        )

    def dp_copy(index):
        other = lax.rem(dp + index, n_dp)
        return remote(
            dp_out.at[pl.ds(other * per_piece, per_piece)], dp_in.at[index - 1],
            s3_send.at[index - 1], s3_recv.at[index - 1], dp=other,
        )

    order = list(range(1, n_chip)) + [0]
    for index in order:
        core_copy(index).start()
    for index in order:
        core_copy(index).wait_recv()
        at = ordered(index) * per_chip
        both = gsum[pl.ds(core * half + at, per_chip)] + core_in[pl.ds(at, per_chip)]
        if index > 0:
            chip_out[index - 1] = both.astype(bf16)
            chip_copy(index).start()
    for index in range(1, n_chip):
        chip_copy(index).wait_recv()
        both += chip_in[index - 1].astype(f32)
    dp_out[...] = both.astype(bf16)
    core_in[pl.ds(0, per_chip)] = both
    for index in range(1, n_dp):
        dp_copy(index).start()
    piece = core_in[pl.ds(dp * per_piece, per_piece)]
    for index in range(1, n_dp):
        dp_copy(index).wait_recv()
        piece += dp_in[index - 1].astype(f32)

    mine = core * half + chip * per_chip
    final[pl.ds(mine + dp * per_piece, per_piece)] = piece.astype(bf16)

    def dp_share(index, start):
        at = final.at[pl.ds(mine + start * per_piece, per_piece)]
        return remote(
            at, at, s4_send.at[index - 1], s4_recv.at[index - 1], dp=lax.rem(dp + index, n_dp)
        )

    def chip_share(index, start):
        at = final.at[pl.ds(core * half + start * per_chip, per_chip)]
        return remote(
            at, at, s5_send.at[index - 1], s5_recv.at[index - 1], seq=2 * ordered(index) + core
        )

    def core_share(index, side):
        at = final.at[
            pl.ds(side * half + lax.rem(chip - index + n_chip, n_chip) * per_chip, per_chip)
        ]
        return remote(at, at, s6_send.at[index], s6_recv.at[index], seq=sibling)

    for index in range(1, n_dp):
        dp_share(index, dp).start()
    for index in range(1, n_dp):
        dp_share(index, lax.rem(dp - index + n_dp, n_dp)).wait_recv()
    for index in range(1, n_chip):
        chip_share(index, chip).start()
    core_share(0, core).start()
    for index in range(1, n_chip):
        chip_share(index, lax.rem(chip - index + n_chip, n_chip)).wait_recv()
        core_share(index, core).start()
    for index in range(n_chip):
        core_share(index, 1 - core).wait_recv()

    for out, start in (
        (out_aq, 0),
        (out_ak, tiles_a),
        (out_av, 2 * tiles_a),
        (out_bq, at_bq),
        (out_bk, at_bk),
        (out_bv, at_bv),
    ):
        for tile in range(out.shape[1] // LANES):
            out[:, tile * LANES : (tile + 1) * LANES] = final[start + tile].astype(f32)

    for chunk in range(chunks):
        @pl.when(seq + 2 < n_seq)
        def _():
            send_two(chunk).wait_send()

        @pl.when(seq + near_hop < n_seq)
        def _():
            send_near(chunk).wait_send()

        @pl.when(chip >= 1)
        def _():
            relay(chunk).wait_send()

    for hop in range(1, HOPS + 1):
        @pl.when(seq + hop < n_seq)
        def _():
            send_low(hop).wait_send()

        @pl.when(seq >= hop)
        def _():
            send_u(hop).wait_send()

    for index in range(n_chip):
        core_copy(index).wait_send()
        core_share(index, core).wait_send()
    for index in range(1, n_chip):
        chip_copy(index).wait_send()
        chip_share(index, chip).wait_send()
    for index in range(1, n_dp):
        dp_copy(index).wait_send()
        dp_share(index, dp).wait_send()


def shards(
    n_seq,
    n_dp,
    normed_input,
    q_base,
    k_base,
    v_base,
    d_attn,
    lengths,
    a_query,
    b_query,
    a_key,
    b_key,
    a_value,
    b_value,
):
    tok, width = normed_input.shape[1:]
    rank = a_query.shape[1]
    q_cols = q_base.shape[2]
    kv_cols = k_base.shape[2]
    groups = kv_cols // HD
    n_chip = n_seq // 2
    span = (HOPS + 1) * tok
    tiles = (3 * width + q_cols + 2 * kv_cols) // LANES
    pieces = n_seq * n_dp
    per_piece = -(-tiles // pieces)
    total = pieces * per_piece
    per_chip = n_dp * per_piece
    half = n_chip * per_chip
    tile = (rank, LANES)
    vmem = pl.BlockSpec(memory_space=pltpu.VMEM)
    dma = pltpu.SemaphoreType.DMA
    flops = 20 * tok * span * q_cols
    outs = pl.pallas_call(
        functools.partial(kernel, n_seq, n_dp, per_piece),
        out_shape=(
            jax.ShapeDtypeStruct((tok, q_cols), bf16),
            jax.ShapeDtypeStruct((rank, width), f32),
            jax.ShapeDtypeStruct((rank, q_cols), f32),
            jax.ShapeDtypeStruct((rank, width), f32),
            jax.ShapeDtypeStruct((rank, kv_cols), f32),
            jax.ShapeDtypeStruct((rank, width), f32),
            jax.ShapeDtypeStruct((rank, kv_cols), f32),
        ),
        in_specs=[vmem] * 5 + [pl.BlockSpec(memory_space=pltpu.SMEM)] + [vmem] * 6,
        out_specs=(vmem,) * 7,
        scratch_shapes=[
            pltpu.VMEM((groups, 2 * tok, HD), bf16),
            pltpu.VMEM((groups, 2 * tok, HD), bf16),
            pltpu.VMEM((groups // 2, span, 4 * HD), bf16),
            pltpu.VMEM((HOPS + 1, 2 * rank, tok), bf16),
            pltpu.VMEM((tok, span), f32),
            pltpu.VMEM((2 * groups, rank, 2 * HD), bf16),
            pltpu.VMEM((groups, rank, 2 * HD), bf16),
            pltpu.VMEM((groups, rank, 2 * HD), bf16),
            pltpu.VMEM((rank, tok), f32),
            pltpu.VMEM((HOPS + 1, 2 * rank, tok), f32),
            pltpu.VMEM((HOPS, 2 * rank, tok), f32),
            pltpu.VMEM((total,) + tile, f32),
            pltpu.VMEM((half,) + tile, f32),
            pltpu.VMEM((n_chip - 1, per_chip) + tile, bf16),
            pltpu.VMEM((n_chip - 1, per_chip) + tile, bf16),
            pltpu.VMEM((per_chip,) + tile, bf16),
            pltpu.VMEM((n_dp - 1, per_piece) + tile, bf16),
            pltpu.VMEM((total,) + tile, bf16),
            dma((groups // 2, 2)),
            dma((groups // 2, HOPS)),
            dma((groups // 2,)),
            dma((HOPS,)),
            dma((HOPS,)),
            dma((HOPS,)),
            dma((HOPS,)),
            dma((n_chip,)),
            dma((n_chip,)),
            dma((n_chip - 1,)),
            dma((n_chip - 1,)),
            dma((n_dp - 1,)),
            dma((n_dp - 1,)),
            dma((n_dp - 1,)),
            dma((n_dp - 1,)),
            dma((n_chip - 1,)),
            dma((n_chip - 1,)),
            dma((n_chip,)),
            dma((n_chip,)),
        ],
        compiler_params=pltpu.CompilerParams(
            collective_id=0, has_side_effects=True, vmem_limit_bytes=48 * 1024 * 1024
        ),
        cost_estimate=pl.CostEstimate(
            flops=flops, bytes_accessed=6 * 1024 * 1024, transcendentals=span * q_cols
        ),
    )(
        normed_input[0],
        q_base[0],
        k_base[0],
        v_base[0],
        d_attn[0],
        lengths,
        a_query.T,
        a_key.T,
        a_value.T,
        b_query,
        b_key,
        b_value,
    )
    return (outs[0][None], outs[1].T, outs[2], outs[3].T, outs[4], outs[5].T, outs[6])


def solution(mesh):
    return jax.shard_map(
        functools.partial(shards, mesh.shape["seq"], mesh.shape["dp"]),
        mesh=mesh,
        in_specs=(
            P("dp", "seq", None),
            P("dp", "seq", None),
            P("dp", "seq", None),
            P("dp", "seq", None),
            P("dp", "seq", None),
            P("dp"),
            P(),
            P(),
            P(),
            P(),
            P(),
            P(),
        ),
        out_specs=(P("dp", "seq", None), P(), P(), P(), P(), P(), P()),
        check_vma=False,
    )
```

time: 275 us -> 71.7 us (0.26)
  waiting for transfers between devices: 140 us -> 0 us
  matrix products: 55.3 us -> 0 us
  Pallas kernels: 0 us -> 54.5 us
  starting transfers between devices: 33.4 us -> 0 us
  between operations: 15.2 us -> 1.31 us
  other arithmetic: 10.2 us -> 0 us
  local copies, waits for them, and re-layouts: 18.8 us -> 15.3 us
    psum x1 -> x0, waiting for transfers between devices: 134 us -> none  [shards(): lax.psum((grad_a_query, grad_b_query, grad_a_key, grad_b_key, grad_a_valu...]
    pallas_call x0 -> x1, Pallas kernels: none -> 54.5 us  [shards(): pl.pallas_call(functools.partial(kernel, n_seq, n_dp, per_piece), out_sha...]
    dot_general x33 -> x0, matrix products: 49.7 us -> none  [the longest x4 10 us: attend(): jnp.einsum('grqk,qgrd->kgd', probs_low, d_out, preferred_element_type=jnp...]
    ppermute x15 -> x0, starting transfers between devices: 33.4 us -> none  [shifted(): lax.ppermute(value, axis, [(source, source + steps) for source in range(l...]
    ppermute x15 -> x0, waiting for transfers between devices: 5.89 us -> none  [shifted(): lax.ppermute(value, axis, [(source, source + steps) for source in range(l...]
    sub x4 -> x0, matrix products: 5.62 us -> none  [attend(): raw_weight = jnp.exp(scores - top_score)]
    unnamed x49 -> x29, local copies, waits for them, and re-layouts: 11.3 us -> 15.3 us
    reshape x6 -> x0, local copies, waits for them, and re-layouts: 3.74 us -> none  [the longest x1 1.33 us: shards(): value_rows.reshape(key_span, groups, 2, HD).transpose(1, 0, 2, 3)]
  transfers between devices with their start and end apart: 16 -> 0, of which waited for: 3 -> 0; matrix products, arithmetic and copies ran while one was open for 5% -> 0% of each run, Pallas kernels for 0% -> 0%
where the time goes in v1:
time: 71.7 us; the launch traced here: 71.1 us
  Pallas kernels  54.5 us (76%)
  local copies, waits for them, and re-layouts  15.3 us (21%)
  between operations  1.31 us (2%)
    pallas_call x1, Pallas kernels, shards(): pl.pallas_call(functools.partial(kernel, n_seq, n_dp, per_piece), out_sha...  54.5 us
    unnamed x29, local copies, waits for them, and re-layouts  15.3 us

profile of v1, /device:TPU:0, one launch (start us, length us, event | category | flops | bytes accessed | tf_op | source)
XLA Modules:
  0.0 71.1 jit_solution(9714916148045844551)
XLA Ops:
  1.3 0.0 copy-start
  1.3 1.3 %copy-done = bf16[1,128,5376]{2,1,0:T(8,128)(2,1)S(1)} copy-done((bf16[1,128,5376]{2,1,0:T(8,128)(2,1)S(1)}, bf16[1,128,5376]{2,1,0:T(8,128)(2,1)}, u32[]{:S(2)}) %copy-start) | copy-done | bytes 1376280
  2.6 0.0 copy-start.1
  2.6 1.0 %copy-done.1 = bf16[1,128,2048]{2,1,0:T(8,128)(2,1)S(1)} copy-done((bf16[1,128,2048]{2,1,0:T(8,128)(2,1)S(1)}, bf16[1,128,2048]{2,1,0:T(8,128)(2,1)}, u32[]{:S(2)}) %copy-start.1) | copy-done | bytes 524312
  3.7 0.0 copy-start.2
  3.7 1.0 %copy-done.2 = bf16[1,128,2048]{2,1,0:T(8,128)(2,1)S(1)} copy-done((bf16[1,128,2048]{2,1,0:T(8,128)(2,1)S(1)}, bf16[1,128,2048]{2,1,0:T(8,128)(2,1)}, u32[]{:S(2)}) %copy-start.2) | copy-done | bytes 524312
  4.7 0.0 copy-start.3
  4.7 0.9 %copy-done.3 = bf16[1,128,1024]{2,1,0:T(8,128)(2,1)S(1)} copy-done((bf16[1,128,1024]{2,1,0:T(8,128)(2,1)S(1)}, bf16[1,128,1024]{2,1,0:T(8,128)(2,1)}, u32[]{:S(2)}) %copy-start.3) | copy-done | bytes 262168
  5.7 0.0 copy-start.4
  5.7 0.9 %copy-done.4 = bf16[1,128,1024]{2,1,0:T(8,128)(2,1)S(1)} copy-done((bf16[1,128,1024]{2,1,0:T(8,128)(2,1)S(1)}, bf16[1,128,1024]{2,1,0:T(8,128)(2,1)}, u32[]{:S(2)}) %copy-start.4) | copy-done | bytes 262168
  6.6 0.0 copy-start.5
  6.6 0.9 %copy-done.5 = bf16[5376,16]{0,1:T(8,128)(2,1)S(1)} copy-done((bf16[5376,16]{0,1:T(8,128)(2,1)S(1)}, bf16[5376,16]{0,1:T(8,128)(2,1)}, u32[]{:S(2)}) %copy-start.5) | copy-done | bytes 172056
  7.5 0.0 copy-start.6
  7.5 0.9 %copy-done.6 = bf16[5376,16]{0,1:T(8,128)(2,1)S(1)} copy-done((bf16[5376,16]{0,1:T(8,128)(2,1)S(1)}, bf16[5376,16]{0,1:T(8,128)(2,1)}, u32[]{:S(2)}) %copy-start.6) | copy-done | bytes 172056
  8.4 0.0 copy-start.7
  8.4 0.9 %copy-done.7 = bf16[5376,16]{0,1:T(8,128)(2,1)S(1)} copy-done((bf16[5376,16]{0,1:T(8,128)(2,1)S(1)}, bf16[5376,16]{0,1:T(8,128)(2,1)}, u32[]{:S(2)}) %copy-start.7) | copy-done | bytes 172056
  9.4 0.0 copy-start.8
  9.4 0.8 %copy-done.8 = bf16[16,2048]{1,0:T(8,128)(2,1)S(1)} copy-done((bf16[16,2048]{1,0:T(8,128)(2,1)S(1)}, bf16[16,2048]{1,0:T(8,128)(2,1)}, u32[]{:S(2)}) %copy-start.8) | copy-done | bytes 65560
  10.2 0.0 copy-start.9
  10.2 0.8 %copy-done.9 = bf16[16,1024]{1,0:T(8,128)(2,1)S(1)} copy-done((bf16[16,1024]{1,0:T(8,128)(2,1)S(1)}, bf16[16,1024]{1,0:T(8,128)(2,1)}, u32[]{:S(2)}) %copy-start.9) | copy-done | bytes 32792
  11.0 0.0 copy-start.10
  11.0 0.8 %copy-done.10 = bf16[16,1024]{1,0:T(8,128)(2,1)S(1)} copy-done((bf16[16,1024]{1,0:T(8,128)(2,1)S(1)}, bf16[16,1024]{1,0:T(8,128)(2,1)}, u32[]{:S(2)}) %copy-start.10) | copy-done | bytes 32792
  11.7 54.5 %shard_map.171 = (bf16[128,2048]{1,0:T(8,128)(2,1)S(1)}, f32[16,5376]{1,0:T(8,128)S(1)}, f32[16,2048]{1,0:T(8,128)S(1)}, f32[16,5376]{1,0:T(8,128)S(1)}, f32[16,...) custom-call(bf16[128,5376]{1,0:T(8,128)(2,1)S(1)} %bitcast.16, bf16[128,2048]{1,0:T(8,128)(2,1)S(1)} %bitcast.17, ...), custom_call_target="tpu_custom_call" | custom-call | flops 2684354560 | bytes 6291456 | tf_op jit(solution)/shard_map/pallas_call | solution.py:526
  66.2 0.8 %copy.27 = bf16[1,128,2048]{2,1,0:T(8,128)(2,1)} copy(bf16[1,128,2048]{2,1,0:T(8,128)(2,1)S(1)} %bitcast.12) | data formatting | bytes 1048576
  67.0 0.7 %copy.28 = f32[5376,16]{0,1:T(8,128)} copy(f32[5376,16]{0,1:T(8,128)S(1)} %bitcast.15) | data formatting | bytes 688128
  67.8 0.7 copy.29
  68.4 0.7 %copy.30 = f32[5376,16]{0,1:T(8,128)} copy(f32[5376,16]{0,1:T(8,128)S(1)} %bitcast.14) | data formatting | bytes 688128
  69.1 0.6 copy.31
  69.8 0.7 %copy.32 = f32[5376,16]{0,1:T(8,128)} copy(f32[5376,16]{0,1:T(8,128)S(1)} %bitcast.13) | data formatting | bytes 688128
  70.5 0.6 copy.33
Async XLA Ops:
  1.3 1.3 %copy-start = (bf16[1,128,5376]{2,1,0:T(8,128)(2,1)S(1)}, bf16[1,128,5376]{2,1,0:T(8,128)(2,1)}, u32[]{:S(2)}) copy-start(bf16[1,128,5376]{2,1,0:T(8,128)(2,1)} %param.12) | copy-start | bytes 4128772
  2.6 1.0 %copy-start.1 = (bf16[1,128,2048]{2,1,0:T(8,128)(2,1)S(1)}, bf16[1,128,2048]{2,1,0:T(8,128)(2,1)}, u32[]{:S(2)}) copy-start(bf16[1,128,2048]{2,1,0:T(8,128)(2,1)} %param.13) | copy-start | bytes 1572868
  3.7 1.0 %copy-start.2 = (bf16[1,128,2048]{2,1,0:T(8,128)(2,1)S(1)}, bf16[1,128,2048]{2,1,0:T(8,128)(2,1)}, u32[]{:S(2)}) copy-start(bf16[1,128,2048]{2,1,0:T(8,128)(2,1)} %param.16) | copy-start | bytes 1572868
  4.7 0.9 %copy-start.3 = (bf16[1,128,1024]{2,1,0:T(8,128)(2,1)S(1)}, bf16[1,128,1024]{2,1,0:T(8,128)(2,1)}, u32[]{:S(2)}) copy-start(bf16[1,128,1024]{2,1,0:T(8,128)(2,1)} %param.14) | copy-start | bytes 786436
  5.7 0.9 %copy-start.4 = (bf16[1,128,1024]{2,1,0:T(8,128)(2,1)S(1)}, bf16[1,128,1024]{2,1,0:T(8,128)(2,1)}, u32[]{:S(2)}) copy-start(bf16[1,128,1024]{2,1,0:T(8,128)(2,1)} %param.15) | copy-start | bytes 786436
  6.6 0.9 %copy-start.5 = (bf16[5376,16]{0,1:T(8,128)(2,1)S(1)}, bf16[5376,16]{0,1:T(8,128)(2,1)}, u32[]{:S(2)}) copy-start(bf16[5376,16]{0,1:T(8,128)(2,1)} %param.18) | copy-start | bytes 516100
  7.5 0.9 %copy-start.6 = (bf16[5376,16]{0,1:T(8,128)(2,1)S(1)}, bf16[5376,16]{0,1:T(8,128)(2,1)}, u32[]{:S(2)}) copy-start(bf16[5376,16]{0,1:T(8,128)(2,1)} %param.20) | copy-start | bytes 516100
  8.4 0.9 %copy-start.7 = (bf16[5376,16]{0,1:T(8,128)(2,1)S(1)}, bf16[5376,16]{0,1:T(8,128)(2,1)}, u32[]{:S(2)}) copy-start(bf16[5376,16]{0,1:T(8,128)(2,1)} %param.22) | copy-start | bytes 516100
  9.4 0.8 %copy-start.8 = (bf16[16,2048]{1,0:T(8,128)(2,1)S(1)}, bf16[16,2048]{1,0:T(8,128)(2,1)}, u32[]{:S(2)}) copy-start(bf16[16,2048]{1,0:T(8,128)(2,1)} %b_query.1) | copy-start | bytes 196612
  10.2 0.8 %copy-start.9 = (bf16[16,1024]{1,0:T(8,128)(2,1)S(1)}, bf16[16,1024]{1,0:T(8,128)(2,1)}, u32[]{:S(2)}) copy-start(bf16[16,1024]{1,0:T(8,128)(2,1)} %b_key.1) | copy-start | bytes 98308
  11.0 0.8 %copy-start.10 = (bf16[16,1024]{1,0:T(8,128)(2,1)S(1)}, bf16[16,1024]{1,0:T(8,128)(2,1)}, u32[]{:S(2)}) copy-start(bf16[16,1024]{1,0:T(8,128)(2,1)} %b_value.1) | copy-start | bytes 98308
